TPU v7x, 768 devices: a whole 4x8x12 slice. The times are simulated.
768 devices in a mesh: dp: 12 (over z), et: 64 (over y, x, core).
Axes of the slice: x: 4, y: 8, z: 12, core: 2. Of those that a mesh axis runs over, the one named last changes fastest.
Arguments:
- hidden_t: bfloat16 [10752, 1536], P('et', 'dp'), may hold values from -6 to 6
- weights: bfloat16 [2, 10752, 6144], P(None, 'et'), may hold values from -0.15625 to 0.15625
- grad_out_t: bfloat16 [6144, 1536], P('et', 'dp'), may hold values from -1.1953125 to 1.1953125
- counts: int32 [12, 2], P('dp'), may hold values from 1 to 96, 128 in all within a row
- row_order: int32 [12, 128], P('dp'), may hold values from 0 to 127, each once within a row
Outputs:
- outputs_t: bfloat16 [6144, 1536], P('et', 'dp')
- grad_hidden_t: bfloat16 [10752, 1536], P('et', 'dp')
- grad_weights: bfloat16 [2, 10752, 6144], P(None, 'et', 'dp')
Inputs may be any that keep to these rules, and one draw needn't show every extreme that they name: Each group's counts sum to 128, and no count exceeds 3 * 32. Each group's row_order is a permutation of its 128 rows.
All inputs are finite; a program needn't handle non-finite values.
Results may differ from a plain program's by a relative error of at most 0.02.
Values may be sent and summed in bfloat16 or wider, within the bound.
A program may use at most 32 MiB of HBM per device.

v0:
```python
import jax
import jax.numpy as jnp
from jax import lax
from jax.sharding import PartitionSpec as P


def routing(counts_row, order_row):
    positions = jnp.arange(order_row.shape[0], dtype=jnp.int32)
    bounds = jnp.cumsum(counts_row)[:-1]
    sorted_expert = jnp.sum((positions[:, None] >= bounds[None, :]).astype(jnp.int32), axis=1)
    return jnp.zeros((order_row.shape[0],), jnp.int32).at[order_row].set(sorted_expert)


def shards(hidden_t, weights, grad_out_t, counts, row_order):
    experts = weights.shape[0]
    local_ff = weights.shape[1]
    model_dim = weights.shape[2]
    row_count = hidden_t.shape[1]
    routed = routing(counts[0], row_order[0])
    chosen = [routed == expert for expert in range(experts)]
    zero = jnp.zeros((), jnp.bfloat16)
    total = jnp.zeros(
        (model_dim // lax.axis_size("et") * lax.axis_size("et"), row_count), jnp.float32
    )
    for project_expert in range(experts):
        part = lax.dot_general(
            weights[project_expert],
            hidden_t,
            (((0,), (0,)), ((), ())),
            preferred_element_type=jnp.float32,
        )
        total = total + jnp.where(chosen[project_expert][None, :], part, 0.0)
    outputs_t = lax.psum_scatter(total, "et", scatter_dimension=0, tiled=True).astype(jnp.bfloat16)
    full_grad = lax.all_gather(grad_out_t, "et", axis=0, tiled=True)
    grad_hidden = jnp.zeros((local_ff, row_count), jnp.float32)
    for expert in range(experts):
        back = jnp.dot(weights[expert], full_grad, preferred_element_type=jnp.float32)
        grad_hidden = grad_hidden + jnp.where(chosen[expert][None, :], back, 0.0)
    grad_hidden_t = grad_hidden.astype(jnp.bfloat16)
    partials = []
    for expert in range(experts):
        masked = jnp.where(chosen[expert][None, :], hidden_t, zero)
        partials.append(
            lax.dot_general(
                masked, full_grad, (((1,), (1,)), ((), ())), preferred_element_type=jnp.float32
            )
        )
    stacked = jnp.stack(partials)
    grad_weights = lax.psum_scatter(
        stacked.astype(jnp.bfloat16), "dp", scatter_dimension=2, tiled=True
    )
    return (outputs_t, grad_hidden_t, grad_weights)


def solution(mesh):
    in_specs = (P("et", "dp"), P(None, "et", None), P("et", "dp"), P("dp", None), P("dp", None))
    out_specs = (P("et", "dp"), P("et", "dp"), P(None, "et", "dp"))
    return jax.shard_map(shards, mesh=mesh, in_specs=in_specs, out_specs=out_specs, check_vma=False)
```

profile of v0, /device:TPU:1, one launch (start us, length us, event | category | flops | bytes accessed | tf_op | source)
XLA Modules:
  0.0 340.0 jit_solution(13762012457925070839)
XLA Ops:
  7.2 0.0 all-gather.2.cloned.1.call-start
  7.2 0.7 all-gather.2.cloned.1.call-update
  7.9 0.0 reduce-scatter.3.cloned.1.call-start
  7.9 0.8 reduce-window.4
  8.8 0.7 fusion.31
  9.5 1.0 scatter_custom_fusion
  10.5 0.0 copy-start
  10.5 0.0 copy-start.3
  10.5 2.8 convolution_select_fusion
  13.3 0.0 copy-done
  13.3 0.0 copy-done.3
  13.3 2.8 fusion
  16.1 0.0 reduce-scatter.3.cloned.1.call-update
  16.2 0.0 reduce-scatter.5.cloned.1.call-start
  16.2 91.4 %all-gather.2.cloned.1.call-done = bf16[6144,128]{1,0:T(8,128)(2,1)} async-done(((bf16[96,128]{1,0:T(8,128)(2,1)}), bf16[6144,128]{1,0:T(8,128)(2,1)}) %all-gather.2.cloned.1.call-update) | async-done | bytes 1572880 | tf_op jit(solution)/shard_map/all_gather | solution.py:34
  107.6 0.0 copy-start.2
  107.6 2.7 fusion.1
  110.3 0.0 copy-done.2
  110.3 1.2 fusion.2
  111.5 2.3 pad_maximum_fusion
  113.7 0.0 reduce-scatter.5.cloned.1.call-update
  113.8 0.0 copy-start.1
  113.8 2.5 fusion.19
  116.3 0.3 copy-done.1
  116.6 1.4 fusion.22
  117.9 146.1 %reduce-scatter.3.cloned.1.call-done = f32[96,128]{1,0:T(8,128)} async-done(((f32[6144,128]{1,0:T(8,128)}), f32[96,128]{1,0:T(8,128)}) %reduce-scatter.3.cloned.1.call-update) | async-done | bytes 49168 | tf_op jit(solution)/shard_map/reduce_scatter | solution.py:33
  264.0 1.4 convert_element_type.14
  265.4 68.0 %reduce-scatter.5.cloned.1.call-done = bf16[2,168,512]{2,1,0:T(8,128)(2,1)} async-done(((bf16[2,168,6144]{2,1,0:T(8,128)(2,1)}), bf16[2,168,512]{2,1,0:T(8,128)(2,1)}) %reduce-scatter.5.cloned.1.call-update) | async-done | bytes 344080 | tf_op jit(solution)/shard_map/reduce_scatter | solution.py:49
  (2 shorter events, 0.0 us)
Async XLA Ops:
  7.2 100.4 %all-gather.2.cloned.1.call-start = ((), (), s32[]{:S(2)}) async-start(), calls=%async_computation.3 | async-start | bytes 1597440 | tf_op jit(solution)/shard_map/all_gather | solution.py:34
  7.9 256.1 %reduce-scatter.3.cloned.1.call-start = ((), (), s32[]{:S(2)}) async-start(), calls=%async_computation.2 | async-start | bytes 3194880 | tf_op jit(solution)/shard_map/reduce_scatter | solution.py:33
  10.5 2.8 copy-start
  10.5 2.8 copy-start.3
  16.2 317.3 %reduce-scatter.5.cloned.1.call-start = ((), (), s32[]{:S(2)}) async-start(), calls=%async_computation.4 | async-start | bytes 4472832 | tf_op jit(solution)/shard_map/reduce_scatter | solution.py:49
  107.6 2.7 copy-start.2
  113.8 2.8 copy-start.1
Sparse Core Ops, SparseCore 0:
  11.9 95.5 all-gather.1
  112.8 151.1 reduce-scatter.2
  267.7 65.6 reduce-scatter.4
where the time goes:
time: 345 us; the launch traced here: 340 us
  waiting for transfers between devices  306 us (89%)
  between operations  13.8 us (4%)
  matrix products  13.4 us (4%)
  other arithmetic  5.21 us (2%)
    reduce_scatter x1, waiting for transfers between devices, shards(): lax.psum_scatter(total, 'et', scatter_dimension=0, tiled=True)  146 us
    all_gather x1, waiting for transfers between devices, shards(): full_grad = lax.all_gather(grad_out_t, 'et', axis=0, tiled=True)  91.4 us
    reduce_scatter x1, waiting for transfers between devices, shards(): lax.psum_scatter(stacked.astype(jnp.bfloat16), 'dp', scatter_dimension=2,...  68 us
  transfers between devices with their start and end apart: 3, of which 3 were waited for; matrix products, arithmetic and copies ran while one was open for 6% of the time, Pallas kernels for 0%

commit v1 on v0

v1 whole, which is shorter than its diff:
```python
import jax
import jax.numpy as jnp
from jax import lax
from jax.experimental import pallas as pl
from jax.experimental.pallas import tpu as pltpu
from jax.sharding import PartitionSpec as P

MESH = pl.DeviceIdType.MESH
NY, NX, NZ = 8, 4, 12
BF16, F32 = jnp.bfloat16, jnp.float32


def dot(a, b, ca, cb):
    return lax.dot_general(a, b, (((ca,), (cb,)), ((), ())), preferred_element_type=F32)


def kernel(
    h_ref, w_hbm, g_ref, counts_ref, order_ref, out_ref, gh_ref, gw_ref,
    w_v, full, gath, hbuf, mbuf, hm, part, sibs, sibr, xs, xr, ys, yr,
    wsem, p_s, p_r, hz_s, hz_r, mz_s, mz_r,
    a1y_s, a1y_r, a1x_s, a1x_r, a1c_s, a1c_r,
    a2y_s, a2y_r, a2x_s, a2x_r, a2c_s, a2c_r,
    rc_s, rc_r, rx_s, rx_r, ry_s, ry_r,
):
    z = lax.axis_index("dp")
    et = lax.axis_index("et")
    y, x, c = et // 8, (et // 2) % 4, et % 2
    kq, ks = z // 3, z % 3

    def dev(yy, xx, cc):
        return (z, (yy * 4 + xx) * 2 + cc)

    def rem(a, n):
        return lax.rem(a + n, n)

    def ypeer(d):
        return dev(rem(y + d, NY), x, c)

    def xpeer(e):
        return dev(y, rem(x + e, NX), c)

    def zpeer(d):
        return (rem(z + d, NZ), et)

    sibling = dev(y, x, 1 - c)

    def remote(src, dst, ss, rs, peer):
        return pltpu.make_async_remote_copy(
            src_ref=src, dst_ref=dst, send_sem=ss, recv_sem=rs, device_id=peer, device_id_type=MESH
        )

    def unit_dest(t):
        u = et * 3 + t
        return u // 16, (u % 16) * 4 + kq

    my_w, my_kq = et // 4, et % 4
    my_u = z * 16 + my_w
    src_et, src_t = my_u // 3, my_u % 3

    def unit_source(s):
        return my_kq * 3 + s, src_et

    def far(n):
        return rem(y + 4 + (1 - 2 * (n % 2)) * ((n + 1) // 2), NY)

    def w_copy(n):
        yy = far(n)
        cols = pl.ds(pl.multiple_of(yy * 768, 768), 768)
        return pltpu.make_async_copy(w_hbm.at[:, :, cols], w_v.at[yy], wsem.at[n])

    for n in range(8):
        w_copy(n).start()

    bar = pltpu.get_barrier_semaphore()

    def greet(peer):
        pl.semaphore_signal(bar, inc=1, device_id=peer, device_id_type=MESH)

    for d in range(1, NY):
        greet(ypeer(d))
    for e in range(1, NX):
        greet(xpeer(e))
    greet(sibling)
    for d in range(1, NZ):
        greet(zpeer(d))

    def is_self(peer):
        return jnp.logical_and(peer[0] == z, peer[1] == et)

    greeted = 7 + 3 + 1 + 11
    for t in range(3):
        for peer in (unit_dest(t), unit_source(t)):
            own = is_self(peer)

            greeted = greeted + jnp.where(own, 0, 1)

            @pl.when(jnp.logical_not(own))
            def _():
                greet(peer)

    order = jnp.broadcast_to(order_ref[...].astype(F32), (128, 128)).T
    lane = lax.broadcasted_iota(jnp.int32, (128, 128), 1).astype(F32)
    pos = lax.broadcasted_iota(jnp.int32, (128, 128), 0)
    expert = (pos >= counts_ref[0, 0]).astype(F32)
    routed = jnp.sum(jnp.where(order == lane, expert, 0.0), axis=0, keepdims=True)
    mbuf[z] = jnp.broadcast_to(routed, (16, 128)).astype(BF16)
    h = h_ref[...]
    hbuf[z] = h
    for k in range(2):
        hm[k] = jnp.where(routed == float(k), h.astype(F32), 0.0).astype(BF16)
    full[y, x, c] = g_ref[...]

    pl.semaphore_wait(bar, greeted)

    def p_copy(t):
        i, j = unit_dest(t)
        w = (et * 3 + t) % 16
        return remote(
            g_ref.at[pl.ds(32 * t, 32)],
            gath.at[kq // 2, kq % 2, ks, w // 2, w % 2],
            p_s.at[t], p_r.at[ks], (i, j),
        )

    for t in range(3):
        peer = unit_dest(t)
        own = is_self(peer)

        @pl.when(jnp.logical_not(own))
        def _():
            p_copy(t).start()

        @pl.when(own)
        def _():
            w = (et * 3 + t) % 16
            gath[kq // 2, kq % 2, ks, w // 2, w % 2] = g_ref[pl.ds(32 * t, 32), :]

    def near(m):
        return ((m + 1) // 2) * (1 - 2 * ((m + 1) % 2))

    def a1y(d):
        return remote(g_ref, full.at[y, x, c], a1y_s.at[d], a1y_r.at[d], ypeer(d))

    def a1y_recv(m):
        d = rem(near(m), NY)
        yy = rem(y - d, NY)
        remote(g_ref, full.at[yy, x, c], a1y_s.at[d], a1y_r.at[d], ypeer(d)).wait_recv()

    def a1x(m, e):
        yy = rem(y - near(m), NY)
        i = m * 4 + e
        return remote(full.at[yy, x, c], full.at[yy, x, c], a1x_s.at[i], a1x_r.at[i], xpeer(e))

    def a1x_recv(m, e):
        yy = rem(y - near(m), NY)
        i = m * 4 + e
        blk = full.at[yy, rem(x - e, NX), c]
        remote(blk, blk, a1x_s.at[i], a1x_r.at[i], xpeer(e)).wait_recv()

    def a1c(m, cc):
        blk = full.at[rem(y - near(m), NY), :, cc]
        return remote(blk, blk, a1c_s.at[m], a1c_r.at[m], sibling)

    def gblk(yy, xx):
        return gath.at[xx % 2, c, :, yy, xx // 2]

    def a2y(d):
        return remote(gblk(y, x), gblk(y, x), a2y_s.at[d], a2y_r.at[d], ypeer(d))

    def a2y_recv(m):
        d = rem(near(m), NY)
        blk = gblk(rem(y - d, NY), x)
        remote(blk, blk, a2y_s.at[d], a2y_r.at[d], ypeer(d)).wait_recv()

    def a2x(m, e):
        blk = gblk(rem(y - near(m), NY), x)
        i = m * 4 + e
        return remote(blk, blk, a2x_s.at[i], a2x_r.at[i], xpeer(e))

    def a2x_recv(m, e):
        blk = gblk(rem(y - near(m), NY), rem(x - e, NX))
        i = m * 4 + e
        remote(blk, blk, a2x_s.at[i], a2x_r.at[i], xpeer(e)).wait_recv()

    def a2c(m, cc):
        blk = gath.at[:, cc, :, rem(y - near(m), NY)]
        return remote(blk, blk, a2c_s.at[m], a2c_r.at[m], sibling)

    def hz(d):
        return remote(h_ref, hbuf.at[z], hz_s.at[d], hz_r.at[d], zpeer(d))

    def hz_recv(d):
        remote(h_ref, hbuf.at[rem(z - d, NZ)], hz_s.at[d], hz_r.at[d], zpeer(d)).wait_recv()

    def mz(d):
        return remote(mbuf.at[z], mbuf.at[z], mz_s.at[d], mz_r.at[d], zpeer(d))

    def mz_recv(d):
        blk = mbuf.at[rem(z - d, NZ)]
        remote(blk, blk, mz_s.at[d], mz_r.at[d], zpeer(d)).wait_recv()

    for d in (4, 3, 5, 2, 6, 1, 7):
        a1y(d).start()
    for d in range(1, NZ):
        hz(d).start()
        mz(d).start()

    def rc(n):
        yy = far(n)
        return remote(sibs.at[yy], sibr.at[yy], rc_s.at[n], rc_r.at[n], sibling)

    def rx(n, e):
        yy = far(n)
        i = n * 4 + e
        return remote(xs.at[yy, rem(x + e, NX)], xr.at[yy, e], rx_s.at[i], rx_r.at[i], xpeer(e))

    def ry(n):
        yy = far(n)
        d = rem(yy - y, NY)
        return remote(ys.at[yy], yr.at[d], ry_s.at[d], ry_r.at[d], dev(yy, x, c))

    def step(n, carry):
        @pl.when(n < 8)
        def _():
            w_copy(n).wait()
            yy = far(n)
            p = dot(w_v[yy, 0], hm[0], 0, 0) + dot(w_v[yy, 1], hm[1], 0, 0)
            part[yy] = p.reshape(4, 2, 96, 128)
            sibs[yy] = part[yy, :, 1 - c].astype(BF16)
            rc(n).start()

        @pl.when(jnp.logical_and(n >= 1, n < 9))
        def _():
            m = n - 1
            yy = far(m)
            rc(m).wait_recv()
            total = part[yy, :, c] + sibr[yy].astype(F32)
            part[yy, :, c] = total
            xs[yy] = total.astype(BF16)
            for e in range(1, NX):
                rx(m, e).start()

        @pl.when(jnp.logical_and(n >= 2, n < 10))
        def _():
            m = n - 2
            yy = far(m)
            total = part[yy, x, c]
            for e in range(1, NX):
                rx(m, e).wait_recv()
                total = total + xr[yy, e].astype(F32)

            @pl.when(m < 7)
            def _():
                ys[yy] = total.astype(BF16)
                ry(m).start()

            @pl.when(m == 7)
            def _():
                part[yy, x, c] = total

        @pl.when(n >= 2)
        def _():
            m = n - 2

            @pl.when(m > 0)
            def _():
                a1y_recv(m)

            for e in range(1, NX):
                a1x(m, e).start()

        @pl.when(n == 6)
        def _():
            for s in range(3):
                own = is_self(unit_source(s))

                @pl.when(jnp.logical_not(own))
                def _():
                    blk = gath.at[my_kq // 2, my_kq % 2, s, my_w // 2, my_w % 2]
                    remote(blk, blk, p_s.at[0], p_r.at[s], sibling).wait_recv()

            for d in (4, 3, 5, 2, 6, 1, 7):
                a2y(d).start()

        return carry

    lax.fori_loop(0, 10, step, 0)

    def step2(m, carry):
        @pl.when(m > 0)
        def _():
            a2y_recv(m)

        for e in range(1, NX):
            a2x(m, e).start()
        for e in range(1, NX):
            a1x_recv(m, e)
        a1c(m, c).start()
        return carry

    lax.fori_loop(0, 8, step2, 0)

    total = part[y, x, c]
    for d in range(1, NY):
        remote(ys.at[y], yr.at[d], ry_s.at[d], ry_r.at[d], ypeer(d)).wait_recv()
        total = total + yr[d].astype(F32)
    out_ref[...] = total.astype(BF16)

    def step3(m, acc):
        a1c(m, 1 - c).wait_recv()
        yy = rem(y - near(m), NY)
        g = full[yy].reshape(768, 128)
        acc = tuple(acc[k] + dot(w_v[yy, k], g, 1, 0) for k in range(2))
        for e in range(1, NX):
            a2x_recv(m, e)
        a2c(m, c).start()
        return acc

    zero = jnp.zeros((168, 128), F32)
    back = lax.fori_loop(0, 8, step3, (zero, zero))
    gh_ref[...] = jnp.where(routed == 0.0, back[0], back[1]).astype(BF16)

    for d in range(1, NZ):
        hz_recv(d)
        mz_recv(d)
    for m in range(8):
        a2c(m, 1 - c).wait_recv()
    for k in range(2):
        hs, gs = [], []
        for i in range(12):
            mask = mbuf[i].astype(F32)[0:1]
            hs.append(jnp.where(mask == float(k), hbuf[i].astype(F32), 0.0).astype(BF16))
            q = i // 3
            gs.append(gath[q // 2, q % 2, i % 3].reshape(512, 128))
        gw_ref[k] = dot(jnp.concatenate(hs, axis=1), jnp.concatenate(gs, axis=1), 1, 1).astype(BF16)

    for t in range(3):

        @pl.when(jnp.logical_not(is_self(unit_dest(t))))
        def _():
            p_copy(t).wait_send()

    for d in range(1, NY):
        a1y(d).wait_send()
        a2y(d).wait_send()
        remote(ys.at[y], yr.at[d], ry_s.at[d], ry_r.at[d], ypeer(d)).wait_send()
    for d in range(1, NZ):
        hz(d).wait_send()
        mz(d).wait_send()

    def drain(m, carry):
        rc(m).wait_send()
        a1c(m, c).wait_send()
        a2c(m, c).wait_send()
        for e in range(1, NX):
            a1x(m, e).wait_send()
            a2x(m, e).wait_send()
            rx(m, e).wait_send()
        return carry

    lax.fori_loop(0, 8, drain, 0)


def shards(hidden_t, weights, grad_out_t, counts, row_order):
    vmem = pl.BlockSpec(memory_space=pltpu.VMEM)
    dma = pltpu.SemaphoreType.DMA
    blocks = (8, 4, 96, 128)
    return pl.pallas_call(
        kernel,
        out_shape=(
            jax.ShapeDtypeStruct((96, 128), BF16),
            jax.ShapeDtypeStruct((168, 128), BF16),
            jax.ShapeDtypeStruct((2, 168, 512), BF16),
        ),
        in_specs=[
            vmem,
            pl.BlockSpec(memory_space=pl.ANY),
            vmem,
            pl.BlockSpec(memory_space=pltpu.SMEM),
            vmem,
        ],
        out_specs=(vmem, vmem, vmem),
        scratch_shapes=[
            pltpu.VMEM((8, 2, 168, 768), BF16),
            pltpu.VMEM((8, 4, 2, 96, 128), BF16),
            pltpu.VMEM((2, 2, 3, 8, 2, 32, 128), BF16),
            pltpu.VMEM((12, 168, 128), BF16),
            pltpu.VMEM((12, 16, 128), BF16),
            pltpu.VMEM((2, 168, 128), BF16),
            pltpu.VMEM((8, 4, 2, 96, 128), F32),
            pltpu.VMEM(blocks, BF16),
            pltpu.VMEM(blocks, BF16),
            pltpu.VMEM(blocks, BF16),
            pltpu.VMEM(blocks, BF16),
            pltpu.VMEM((8, 96, 128), BF16),
            pltpu.VMEM((8, 96, 128), BF16),
            dma((8,)), dma((3,)), dma((3,)), dma((12,)), dma((12,)), dma((12,)), dma((12,)),
            dma((8,)), dma((8,)), dma((32,)), dma((32,)), dma((8,)), dma((8,)),
            dma((8,)), dma((8,)), dma((32,)), dma((32,)), dma((8,)), dma((8,)),
            dma((8,)), dma((8,)), dma((32,)), dma((32,)), dma((8,)), dma((8,)),
        ],
        compiler_params=pltpu.CompilerParams(
            collective_id=0, has_side_effects=True, vmem_limit_bytes=48 << 20
        ),
        name="moe_down",
    )(hidden_t, weights, grad_out_t, counts, row_order)


def solution(mesh):
    in_specs = (P("et", "dp"), P(None, "et", None), P("et", "dp"), P("dp", None), P("dp", None))
    out_specs = (P("et", "dp"), P("et", "dp"), P(None, "et", "dp"))
    return jax.shard_map(shards, mesh=mesh, in_specs=in_specs, out_specs=out_specs, check_vma=False)
```

time: 345 us -> 67.1 us (0.19); the launches traced: 340 us -> 66.2 us
  waiting for transfers between devices: 306 us -> 0 us
  Pallas kernels: 0 us -> 58.6 us
  matrix products: 13.4 us -> 0 us
  between operations: 13.8 us -> 0.65 us
  local copies, waits for them, and re-layouts: 1.27 us -> 6.95 us
  other arithmetic: 5.21 us -> 0 us
    reduce_scatter x2 -> x0, waiting for transfers between devices: 214 us -> none  [the longest x1 146 us: shards(): lax.psum_scatter(total, 'et', scatter_dimension=0, tiled=True)]
    all_gather x1 -> x0, waiting for transfers between devices: 91.4 us -> none  [shards(): full_grad = lax.all_gather(grad_out_t, 'et', axis=0, tiled=True)]
    pallas_call x0 -> x1, Pallas kernels: none -> 58.6 us  [shards(): pl.pallas_call(kernel, out_shape=(jax.ShapeDtypeStruct((96, 128), BF16),...]
    dot_general x6 -> x0, matrix products: 13.4 us -> none  [the longest x2 5.61 us: shards(): lax.dot_general(weights[project_expert], hidden_t, (((0,), (0,)), ((), ()...]
    unnamed x8 -> x13, local copies, waits for them, and re-layouts: 0.3 us -> 6.95 us
  transfers between devices with their start and end apart: 3 -> 0, of which waited for: 3 -> 0; matrix products, arithmetic and copies ran while one was open for 6% -> 0% of each run, Pallas kernels for 0% -> 0%
where the time goes in v1:
time: 67.1 us; the launch traced here: 66.2 us
  Pallas kernels  58.6 us (87%)
  local copies, waits for them, and re-layouts  6.95 us (10%)
    pallas_call x1, Pallas kernels, shards(): pl.pallas_call(kernel, out_shape=(jax.ShapeDtypeStruct((96, 128), BF16),...  58.6 us
    unnamed x13, local copies, waits for them, and re-layouts  6.95 us

profile of v1, /device:TPU:1, one launch (start us, length us, event | category | flops | bytes accessed | tf_op | source)
XLA Modules:
  0.0 66.2 jit_solution(5639747204171397092)
XLA Ops:
  0.6 0.0 copy-start
  0.6 2.2 %copy-done = bf16[2,168,6144]{2,1,0:T(8,128)(2,1)S(1)} copy-done((bf16[2,168,6144]{2,1,0:T(8,128)(2,1)S(1)}, bf16[2,168,6144]{2,1,0:T(8,128)(2,1)}, u32[]{:S(2)}) %copy-start) | copy-done | bytes 4128792
  2.8 0.0 copy-start.1
  2.8 0.8 %copy-done.1 = bf16[168,128]{1,0:T(8,128)(2,1)S(1)} copy-done((bf16[168,128]{1,0:T(8,128)(2,1)S(1)}, bf16[168,128]{1,0:T(8,128)(2,1)}, u32[]{:S(2)}) %copy-start.1) | copy-done | bytes 43032
  3.6 0.0 copy-start.2
  3.6 0.7 %copy-done.2 = bf16[96,128]{1,0:T(8,128)(2,1)S(1)} copy-done((bf16[96,128]{1,0:T(8,128)(2,1)S(1)}, bf16[96,128]{1,0:T(8,128)(2,1)}, u32[]{:S(2)}) %copy-start.2) | copy-done | bytes 24600
  4.3 0.0 copy-start.3
  4.3 0.7 copy-done.3
  5.0 0.0 copy-start.4
  5.0 0.7 copy-done.4
  5.6 58.6 %moe_down.1 = (bf16[96,128]{1,0:T(8,128)(2,1)S(1)}, bf16[168,128]{1,0:T(8,128)(2,1)S(1)}, bf16[2,168,512]{2,1,0:T(8,128)(2,1)S(1)}) custom-call(bf16[168,128]{1,0:T(8,128)(2,1)S(1)} %copy-done.1, bf16[2,168,6144]{2,1,0:T(8,128)(2,1)S(1)} %copy-done, bf16[96,128]{1,0:T(8,128)(2,1)S(1)} %copy-done.2, s32[1,2]{1,0:T(1,128)S(1)} %copy-done.3, s32[1,128]{1,0:T(1,128)S(1)} %copy-done.4), custom_call_target="tpu_custom_call" | custom-call | tf_op jit(solution)/shard_map/moe_down/pallas_call | solution.py:367
  64.2 0.6 copy.11
  64.8 0.6 copy.12
  65.5 0.7 %copy.13 = bf16[2,168,512]{2,1,0:T(8,128)(2,1)} copy(bf16[2,168,512]{2,1,0:T(8,128)(2,1)S(1)} %get-tuple-element.8) | data formatting | bytes 688128
Async XLA Ops:
  0.6 2.2 %copy-start = (bf16[2,168,6144]{2,1,0:T(8,128)(2,1)S(1)}, bf16[2,168,6144]{2,1,0:T(8,128)(2,1)}, u32[]{:S(2)}) copy-start(bf16[2,168,6144]{2,1,0:T(8,128)(2,1)} %w_hbm.1) | copy-start | bytes 12386308
  2.8 0.8 %copy-start.1 = (bf16[168,128]{1,0:T(8,128)(2,1)S(1)}, bf16[168,128]{1,0:T(8,128)(2,1)}, u32[]{:S(2)}) copy-start(bf16[168,128]{1,0:T(8,128)(2,1)} %h_ref.1) | copy-start | bytes 129028
  3.6 0.7 %copy-start.2 = (bf16[96,128]{1,0:T(8,128)(2,1)S(1)}, bf16[96,128]{1,0:T(8,128)(2,1)}, u32[]{:S(2)}) copy-start(bf16[96,128]{1,0:T(8,128)(2,1)} %g_ref.1) | copy-start | bytes 73732
  4.3 0.7 copy-start.3
  5.0 0.7 copy-start.4

commit v2 on v0

v2 whole, which is shorter than its diff:
```python
import jax
import jax.numpy as jnp
from jax import lax
from jax.experimental import pallas as pl
from jax.experimental.pallas import tpu as pltpu
from jax.sharding import PartitionSpec as P

MESH = pl.DeviceIdType.MESH
NY, NX, NZ = 8, 4, 12
BF16, F32 = jnp.bfloat16, jnp.float32


def dot(a, b, ca, cb):
    return lax.dot_general(a, b, (((ca,), (cb,)), ((), ())), preferred_element_type=F32)


def kernel(
    h_hbm, w_hbm, g_hbm, counts_hbm, order_hbm, out_ref, gh_ref, gw_ref,
    w_v, full, gath, hbuf, mbuf, hm, part, sibs, sibr, xs, xr, ys, yr, back, hcat, counts_v, order_v,
    wsem, in_sem, p_s, p_r, hz_s, hz_r, mz_s, mz_r,
    a1y_s, a1y_r, a1x_s, a1x_r, a1c_s, a1c_r,
    a2y_s, a2y_r, a2x_s, a2x_r, a2c_s, a2c_r,
    rc_s, rc_r, rx_s, rx_r, ry_s, ry_r,
):
    z = lax.axis_index("dp")
    et = lax.axis_index("et")
    y, x, c = et // 8, (et // 2) % 4, et % 2
    kq, ks = z // 3, z % 3

    def dev(yy, xx, cc):
        return (z, (yy * 4 + xx) * 2 + cc)

    def rem(a, n):
        return lax.rem(a + n, n)

    def ypeer(d):
        return dev(rem(y + d, NY), x, c)

    def xpeer(e):
        return dev(y, rem(x + e, NX), c)

    def zpeer(d):
        return (rem(z + d, NZ), et)

    sibling = dev(y, x, 1 - c)

    def remote(src, dst, ss, rs, peer):
        return pltpu.make_async_remote_copy(
            src_ref=src, dst_ref=dst, send_sem=ss, recv_sem=rs, device_id=peer, device_id_type=MESH
        )

    def unit_dest(t):
        u = et * 3 + t
        return u // 16, (u % 16) * 4 + kq

    my_w, my_kq = et // 4, et % 4
    src_et = (z * 16 + my_w) // 3

    def unit_source(s):
        return my_kq * 3 + s, src_et

    def far(n):
        return rem(y + 4 + (1 - 2 * (n % 2)) * ((n + 1) // 2), NY)

    def near(m):
        return ((m + 1) // 2) * (1 - 2 * ((m + 1) % 2))

    def side(m):
        return 1 - 2 * (m % 2)

    bar = pltpu.get_barrier_semaphore()

    def greet(peer):
        pl.semaphore_signal(bar, inc=1, device_id=peer, device_id_type=MESH)

    def is_self(peer):
        return jnp.logical_and(peer[0] == z, peer[1] == et)

    greeted = 7 + 2 + 1 + 6
    for t in range(3):
        for peer in (unit_dest(t), unit_source(t)):
            own = is_self(peer)
            greeted = greeted + jnp.where(own, 0, 1)

            @pl.when(jnp.logical_not(own))
            def _():
                greet(peer)

    for d in (4, 3, 5, 2, 6, 1, 7):
        greet(ypeer(d))
    for d in (3, -3, 2, -2, 1, -1):
        greet(zpeer(d))
    for e in (1, -1):
        greet(xpeer(e))
    greet(sibling)

    inputs = [
        pltpu.make_async_copy(src, dst, in_sem.at[i])
        for i, (src, dst) in enumerate(
            [
                (order_hbm, order_v),
                (counts_hbm, counts_v),
                (h_hbm, hbuf.at[z]),
                (g_hbm, full.at[y, x, c]),
            ]
        )
    ]
    for copy in inputs:
        copy.start()

    def w_copy(n):
        yy = far(n)
        cols = pl.ds(pl.multiple_of(yy * 768, 768), 768)
        return pltpu.make_async_copy(w_hbm.at[:, :, cols], w_v.at[yy], wsem.at[n])

    for n in range(8):
        w_copy(n).start()
    for copy in inputs:
        copy.wait()

    order = jnp.broadcast_to(order_v[...].astype(F32), (128, 128)).T
    lane = lax.broadcasted_iota(jnp.int32, (128, 128), 1).astype(F32)
    pos = lax.broadcasted_iota(jnp.int32, (128, 128), 0)
    expert = (pos >= counts_v[0:1, 0:1]).astype(F32)
    routed = jnp.sum(jnp.where(order == lane, expert, 0.0), axis=0, keepdims=True)
    mbuf[z] = jnp.broadcast_to(routed, (16, 128)).astype(BF16)
    h = hbuf[z].astype(F32)
    for k in range(2):
        hm[k] = jnp.where(routed == float(k), h, 0.0).astype(BF16)
        back[k] = jnp.zeros((168, 128), F32)

    pl.semaphore_wait(bar, greeted)

    g_own = full.at[y, x, c]

    def p_copy(t):
        w = (et * 3 + t) % 16
        return remote(
            full.at[y, x, c, pl.ds(32 * t, 32)],
            gath.at[kq // 2, kq % 2, ks, w // 2, w % 2],
            p_s.at[t], p_r.at[ks], unit_dest(t),
        )

    for t in range(3):
        own = is_self(unit_dest(t))

        @pl.when(jnp.logical_not(own))
        def _():
            p_copy(t).start()

        @pl.when(own)
        def _():
            w = (et * 3 + t) % 16
            gath[kq // 2, kq % 2, ks, w // 2, w % 2] = full[y, x, c, pl.ds(32 * t, 32), :]

    class Gather:
        def __init__(self, block, pair, sems):
            self.block, self.pair = block, pair
            self.ys, self.yr, self.xs, self.xr, self.cs, self.cr = sems

        def at(self, m, e):
            return self.block(rem(y - near(m), NY), rem(x + e, NX))

        def y_send(self, d):
            blk = self.block(y, x)
            return remote(blk, blk, self.ys.at[d], self.yr.at[d], ypeer(d))

        def y_recv(self, m):
            d = rem(near(m), NY)
            blk = self.at(m, 0)
            remote(blk, blk, self.ys.at[d], self.yr.at[d], ypeer(d)).wait_recv()

        def x_copy(self, m, e, i, to):
            blk = self.at(m, e)
            return remote(blk, blk, self.xs.at[m * 4 + i], self.xr.at[m * 4 + i], xpeer(to))

        def forward(self, m):
            @pl.when(m > 0)
            def _():
                self.y_recv(m)

            self.x_copy(m, 0, 0, 1).start()
            self.x_copy(m, 0, 1, -1).start()

        def relay(self, m):
            s = side(m)
            self.x_copy(m, -s, m % 2, s).wait_recv()
            self.x_copy(m, -s, 2, s).start()

        def finish(self, m):
            s = side(m)
            self.x_copy(m, s, 1 - m % 2, s).wait_recv()
            self.x_copy(m, 2, 2, s).wait_recv()
            self.c_copy(m, c).start()

        def c_copy(self, m, cc):
            blk = self.pair(rem(y - near(m), NY), cc)
            return remote(blk, blk, self.cs.at[m], self.cr.at[m], sibling)

        def drain(self, m):
            s = side(m)
            self.x_copy(m, 0, 0, 1).wait_send()
            self.x_copy(m, 0, 1, -1).wait_send()
            self.x_copy(m, -s, 2, s).wait_send()
            self.c_copy(m, c).wait_send()

    rows = Gather(
        lambda yy, xx: full.at[yy, xx, c],
        lambda yy, cc: full.at[yy, :, cc],
        (a1y_s, a1y_r, a1x_s, a1x_r, a1c_s, a1c_r),
    )
    plane = Gather(
        lambda yy, xx: gath.at[xx % 2, c, :, yy, xx // 2],
        lambda yy, cc: gath.at[:, cc, :, yy],
        (a2y_s, a2y_r, a2x_s, a2x_r, a2c_s, a2c_r),
    )

    for d in (4, 3, 5, 2, 6, 1, 7):
        rows.y_send(d).start()

    def hz(d, to, i):
        k = rem(z + d, NZ)
        return remote(hbuf.at[k], hbuf.at[k], hz_s.at[i], hz_r.at[i], zpeer(to))

    def mz(d, to, i):
        k = rem(z + d, NZ)
        return remote(mbuf.at[k], mbuf.at[k], mz_s.at[i], mz_r.at[i], zpeer(to))

    direct = [(0, d, d % 12) for d in (3, -3, 2, -2, 1, -1)]
    relays = [(-3, d, d + 3) for d in (1, 2, 3)] + [(3, -d, 9 - d) for d in (1, 2)]

    def z_start(hops):
        for d, to, i in hops:
            hz(d, to, i).start()
            mz(d, to, i).start()

    def z_recv(i):
        hz(-i, 1, i).wait_recv()
        mz(-i, 1, i).wait_recv()

    z_start(direct)

    def rc(n):
        yy = far(n)
        return remote(sibs.at[yy], sibr.at[yy], rc_s.at[n], rc_r.at[n], sibling)

    def rx(n, i):
        yy, s = far(n), side(n)
        e, to = ((2, s), (-s, -s), (s, s))[i]
        j = n * 4 + i
        return remote(xs.at[yy, rem(x + e, NX)], xr.at[yy, i], rx_s.at[j], rx_r.at[j], xpeer(to))

    def ry(n):
        yy = far(n)
        d = rem(yy - y, NY)
        return remote(ys.at[yy], yr.at[d], ry_s.at[d], ry_r.at[d], dev(yy, x, c))

    def ryf(d):
        return remote(ys.at[y], yr.at[d], ry_s.at[d], ry_r.at[d], ypeer(d))

    def project(n):
        w_copy(n).wait()
        yy = far(n)
        p = dot(w_v[yy, 0], hm[0], 0, 0) + dot(w_v[yy, 1], hm[1], 0, 0)
        part[yy] = p.reshape(4, 2, 96, 128)
        sibs[yy] = part[yy, :, 1 - c].astype(BF16)
        rc(n).start()

    def chip_sum(n):
        yy = far(n)
        rc(n).wait_recv()
        total = part[yy, :, c] + sibr[yy].astype(F32)
        part[yy, :, c] = total
        xs[yy] = total.astype(BF16)
        rx(n, 0).start()
        rx(n, 1).start()

    def x_relay(n):
        yy = far(n)
        e = rem(x + side(n), NX)
        rx(n, 0).wait_recv()
        xs[yy, e] = (part[yy, e, c] + xr[yy, 0].astype(F32)).astype(BF16)
        rx(n, 2).start()

    def x_sum(n):
        yy = far(n)
        rx(n, 1).wait_recv()
        rx(n, 2).wait_recv()
        total = part[yy, x, c] + xr[yy, 1].astype(F32) + xr[yy, 2].astype(F32)

        @pl.when(n < 7)
        def _():
            ys[yy] = total.astype(BF16)
            ry(n).start()

        @pl.when(n == 7)
        def _():
            part[yy, x, c] = total

    def grad_hidden(m):
        rows.c_copy(m, 1 - c).wait_recv()
        yy = rem(y - near(m), NY)
        g = full[yy].reshape(768, 128)
        for k in range(2):
            back[k] += dot(w_v[yy, k], g, 1, 0)

    def plane_start(m):
        for s in range(3):

            @pl.when(jnp.logical_not(is_self(unit_source(s))))
            def _():
                blk = gath.at[my_kq // 2, my_kq % 2, s, my_w // 2, my_w % 2]
                remote(blk, blk, p_s.at[0], p_r.at[s], sibling).wait_recv()

        for d in (4, 3, 5, 2, 6, 1, 7):
            plane.y_send(d).start()

    def z_relay(m):
        z_recv(3)
        z_recv(9)
        z_start(relays)

    stages = [
        (0, 8, project),
        (1, 8, chip_sum),
        (2, 8, rows.forward),
        (3, 8, x_relay),
        (4, 8, rows.relay),
        (5, 8, x_sum),
        (6, 8, rows.finish),
        (6, 1, plane_start),
        (7, 1, z_relay),
        (8, 8, plane.forward),
        (10, 8, plane.relay),
        (12, 8, plane.finish),
        (10, 8, grad_hidden),
    ]

    def step(n, carry):
        for first, count, stage in stages:

            @pl.when(jnp.logical_and(n >= first, n < first + count))
            def _():
                stage(n - first)

        return carry

    lax.fori_loop(0, max(first + count for first, count, _ in stages), step, 0)

    gh_ref[...] = jnp.where(routed == 0.0, back[0], back[1]).astype(BF16)

    total = part[y, x, c]
    for d in range(1, NY):
        ryf(d).wait_recv()
        total = total + yr[d].astype(F32)
    out_ref[...] = total.astype(BF16)

    for i in (1, 2, 10, 11, 4, 5, 6, 7, 8):
        z_recv(i)
    for i in range(12):
        mask = mbuf[i].astype(F32)[0:1]
        hi = hbuf[i].astype(F32)
        for k in range(2):
            hcat[k, :, 128 * i : 128 * i + 128] = jnp.where(mask == float(k), hi, 0.0).astype(BF16)
    for m in range(8):
        plane.c_copy(m, 1 - c).wait_recv()
    gs = [gath[i // 6, (i // 3) % 2, i % 3].reshape(512, 128) for i in range(12)]
    gs = jnp.concatenate(gs, axis=1)
    for k in range(2):
        gw_ref[k] = dot(hcat[k], gs, 1, 1).astype(BF16)

    for t in range(3):

        @pl.when(jnp.logical_not(is_self(unit_dest(t))))
        def _():
            p_copy(t).wait_send()

    for d in range(1, NY):
        rows.y_send(d).wait_send()
        plane.y_send(d).wait_send()
        ryf(d).wait_send()
    for d, to, i in direct + relays:
        hz(d, to, i).wait_send()
        mz(d, to, i).wait_send()

    def drain(m, carry):
        rc(m).wait_send()
        rows.drain(m)
        plane.drain(m)
        for i in range(3):
            rx(m, i).wait_send()
        return carry

    lax.fori_loop(0, 8, drain, 0)


def shards(hidden_t, weights, grad_out_t, counts, row_order):
    vmem = pl.BlockSpec(memory_space=pltpu.VMEM)
    dma = pltpu.SemaphoreType.DMA
    blocks = (8, 4, 96, 128)
    return pl.pallas_call(
        kernel,
        out_shape=(
            jax.ShapeDtypeStruct((96, 128), BF16),
            jax.ShapeDtypeStruct((168, 128), BF16),
            jax.ShapeDtypeStruct((2, 168, 512), BF16),
        ),
        in_specs=[pl.BlockSpec(memory_space=pl.ANY)] * 5,
        out_specs=(vmem, vmem, vmem),
        scratch_shapes=[
            pltpu.VMEM((8, 2, 168, 768), BF16),
            pltpu.VMEM((8, 4, 2, 96, 128), BF16),
            pltpu.VMEM((2, 2, 3, 8, 2, 32, 128), BF16),
            pltpu.VMEM((12, 168, 128), BF16),
            pltpu.VMEM((12, 16, 128), BF16),
            pltpu.VMEM((2, 168, 128), BF16),
            pltpu.VMEM((8, 4, 2, 96, 128), F32),
            pltpu.VMEM(blocks, BF16),
            pltpu.VMEM(blocks, BF16),
            pltpu.VMEM(blocks, BF16),
            pltpu.VMEM(blocks, BF16),
            pltpu.VMEM((8, 96, 128), BF16),
            pltpu.VMEM((8, 96, 128), BF16),
            pltpu.VMEM((2, 168, 128), F32),
            pltpu.VMEM((2, 168, 1536), BF16),
            pltpu.VMEM((1, 2), jnp.int32),
            pltpu.VMEM((1, 128), jnp.int32),
            dma((8,)), dma((4,)), dma((3,)), dma((3,)), dma((12,)), dma((12,)), dma((12,)), dma((12,)),
            dma((8,)), dma((8,)), dma((32,)), dma((32,)), dma((8,)), dma((8,)),
            dma((8,)), dma((8,)), dma((32,)), dma((32,)), dma((8,)), dma((8,)),
            dma((8,)), dma((8,)), dma((32,)), dma((32,)), dma((8,)), dma((8,)),
        ],
        compiler_params=pltpu.CompilerParams(
            collective_id=0, has_side_effects=True, vmem_limit_bytes=48 << 20
        ),
        name="moe_down",
    )(hidden_t, weights, grad_out_t, counts, row_order)


def solution(mesh):
    in_specs = (P("et", "dp"), P(None, "et", None), P("et", "dp"), P("dp", None), P("dp", None))
    out_specs = (P("et", "dp"), P("et", "dp"), P(None, "et", "dp"))
    return jax.shard_map(shards, mesh=mesh, in_specs=in_specs, out_specs=out_specs, check_vma=False)
```

time: 345 us -> 66.1 us (0.19); the launches traced: 340 us -> 65.8 us
  waiting for transfers between devices: 306 us -> 0 us
  Pallas kernels: 0 us -> 58.2 us
  matrix products: 13.4 us -> 0 us
  between operations: 13.8 us -> 0.65 us
  local copies, waits for them, and re-layouts: 1.27 us -> 6.95 us
  other arithmetic: 5.21 us -> 0 us
    reduce_scatter x2 -> x0, waiting for transfers between devices: 214 us -> none  [the longest x1 146 us: shards(): lax.psum_scatter(total, 'et', scatter_dimension=0, tiled=True)]
    all_gather x1 -> x0, waiting for transfers between devices: 91.4 us -> none  [shards(): full_grad = lax.all_gather(grad_out_t, 'et', axis=0, tiled=True)]
    pallas_call x0 -> x1, Pallas kernels: none -> 58.2 us  [shards(): pl.pallas_call(kernel, out_shape=(jax.ShapeDtypeStruct((96, 128), BF16),...]
    dot_general x6 -> x0, matrix products: 13.4 us -> none  [the longest x2 5.61 us: shards(): lax.dot_general(weights[project_expert], hidden_t, (((0,), (0,)), ((), ()...]
    unnamed x8 -> x13, local copies, waits for them, and re-layouts: 0.3 us -> 6.95 us
  transfers between devices with their start and end apart: 3 -> 0, of which waited for: 3 -> 0; matrix products, arithmetic and copies ran while one was open for 6% -> 0% of each run, Pallas kernels for 0% -> 0%
where the time goes in v2:
time: 66.1 us; the launch traced here: 65.8 us
  Pallas kernels  58.2 us (88%)
  local copies, waits for them, and re-layouts  6.95 us (11%)
    pallas_call x1, Pallas kernels, shards(): pl.pallas_call(kernel, out_shape=(jax.ShapeDtypeStruct((96, 128), BF16),...  58.2 us
    unnamed x13, local copies, waits for them, and re-layouts  6.95 us

profile of v2, /device:TPU:1, one launch (start us, length us, event | category | flops | bytes accessed | tf_op | source)
XLA Modules:
  0.0 65.8 jit_solution(15561911917516195966)
XLA Ops:
  0.6 0.0 copy-start
  0.6 2.2 %copy-done = bf16[2,168,6144]{2,1,0:T(8,128)(2,1)S(1)} copy-done((bf16[2,168,6144]{2,1,0:T(8,128)(2,1)S(1)}, bf16[2,168,6144]{2,1,0:T(8,128)(2,1)}, u32[]{:S(2)}) %copy-start) | copy-done | bytes 4128792
  2.8 0.0 copy-start.1
  2.8 0.8 %copy-done.1 = bf16[168,128]{1,0:T(8,128)(2,1)S(1)} copy-done((bf16[168,128]{1,0:T(8,128)(2,1)S(1)}, bf16[168,128]{1,0:T(8,128)(2,1)}, u32[]{:S(2)}) %copy-start.1) | copy-done | bytes 43032
  3.6 0.0 copy-start.2
  3.6 0.7 %copy-done.2 = bf16[96,128]{1,0:T(8,128)(2,1)S(1)} copy-done((bf16[96,128]{1,0:T(8,128)(2,1)S(1)}, bf16[96,128]{1,0:T(8,128)(2,1)}, u32[]{:S(2)}) %copy-start.2) | copy-done | bytes 24600
  4.3 0.0 copy-start.3
  4.3 0.7 copy-done.3
  5.0 0.0 copy-start.4
  5.0 0.7 copy-done.4
  5.6 58.2 %moe_down.1 = (bf16[96,128]{1,0:T(8,128)(2,1)S(1)}, bf16[168,128]{1,0:T(8,128)(2,1)S(1)}, bf16[2,168,512]{2,1,0:T(8,128)(2,1)S(1)}) custom-call(bf16[168,128]{1,0:T(8,128)(2,1)S(1)} %copy-done.1, bf16[2,168,6144]{2,1,0:T(8,128)(2,1)S(1)} %copy-done, bf16[96,128]{1,0:T(8,128)(2,1)S(1)} %copy-done.2, s32[1,2]{1,0:T(1,128)S(1)} %copy-done.3, s32[1,128]{1,0:T(1,128)S(1)} %copy-done.4), custom_call_target="tpu_custom_call" | custom-call | tf_op jit(solution)/shard_map/moe_down/pallas_call | solution.py:401
  63.8 0.6 copy.11
  64.4 0.6 copy.12
  65.1 0.7 %copy.13 = bf16[2,168,512]{2,1,0:T(8,128)(2,1)} copy(bf16[2,168,512]{2,1,0:T(8,128)(2,1)S(1)} %get-tuple-element.8) | data formatting | bytes 688128
Async XLA Ops:
  0.6 2.2 %copy-start = (bf16[2,168,6144]{2,1,0:T(8,128)(2,1)S(1)}, bf16[2,168,6144]{2,1,0:T(8,128)(2,1)}, u32[]{:S(2)}) copy-start(bf16[2,168,6144]{2,1,0:T(8,128)(2,1)} %w_hbm.1) | copy-start | bytes 12386308
  2.8 0.8 %copy-start.1 = (bf16[168,128]{1,0:T(8,128)(2,1)S(1)}, bf16[168,128]{1,0:T(8,128)(2,1)}, u32[]{:S(2)}) copy-start(bf16[168,128]{1,0:T(8,128)(2,1)} %h_hbm.1) | copy-start | bytes 129028
  3.6 0.7 %copy-start.2 = (bf16[96,128]{1,0:T(8,128)(2,1)S(1)}, bf16[96,128]{1,0:T(8,128)(2,1)}, u32[]{:S(2)}) copy-start(bf16[96,128]{1,0:T(8,128)(2,1)} %g_hbm.1) | copy-start | bytes 73732
  4.3 0.7 copy-start.3
  5.0 0.7 copy-start.4

commit v3 on v2

--- a/solution.py
+++ b/solution.py
@@ -16,8 +16,8 @@
 
 def kernel(
     h_hbm, w_hbm, g_hbm, counts_hbm, order_hbm, out_ref, gh_ref, gw_ref,
-    w_v, full, gath, hbuf, mbuf, hm, part, sibs, sibr, xs, xr, ys, yr, back, hcat, counts_v, order_v,
-    wsem, in_sem, p_s, p_r, hz_s, hz_r, mz_s, mz_r,
+    w_v, full, gath, hbuf, h_v, hm, part, sibs, sibr, xs, xr, ys, yr, back, hcat, gwt, counts_v, order_v,
+    wsem, in_sem, p_s, p_r, hz_s, hz_r,
     a1y_s, a1y_r, a1x_s, a1x_r, a1c_s, a1c_r,
     a2y_s, a2y_r, a2x_s, a2x_r, a2c_s, a2c_r,
     rc_s, rc_r, rx_s, rx_r, ry_s, ry_r,
@@ -25,7 +25,6 @@
     z = lax.axis_index("dp")
     et = lax.axis_index("et")
     y, x, c = et // 8, (et // 2) % 4, et % 2
-    kq, ks = z // 3, z % 3
 
     def dev(yy, xx, cc):
         return (z, (yy * 4 + xx) * 2 + cc)
@@ -49,15 +48,52 @@
             src_ref=src, dst_ref=dst, send_sem=ss, recv_sem=rs, device_id=peer, device_id_type=MESH
         )
 
+    def corner(i):
+        chip = i * 16 // 6
+        return chip // 4, rem(chip % 4 - jnp.where(i % 3 == 0, 1, 0), NX)
+
+    def groups_of(k, i):
+        rel = rem(k - i, NZ) + 1
+        return (rel // 3) % 4, rel % 3
+
+    def group(i, q, s):
+        return (i + 3 * q + s + 11) % NZ
+
+    def place(i, w, q):
+        yc, xc = corner(i)
+        xo, b, cc = w // 8 * 2 + w // 2 % 2, w // 4 % 2, w % 2
+        rank = jnp.where(q == 0, 3, jnp.where(q == 3, 2, 2 - q))
+        yy = (yc + jnp.where(b == 1, 1 + rank, 8 - rank)) % NY
+        return (yy * 4 + (xc + xo) % NX) * 2 + cc
+
+    def row_of(i, yy):
+        dy = rem(yy - corner(i)[0], NY)
+        b = (dy + 3) % 8 // 4
+        rank = jnp.where(b == 1, dy - 1, (8 - dy) % 8)
+        return jnp.where(rank == 3, 0, jnp.where(rank == 2, 3, 2 - rank)), b
+
+    def col_of(i, xx):
+        return rem(xx - corner(i)[1], NX)
+
+    def unit(t):
+        u = et * 3 + t
+        return u // 16, u % 16
+
     def unit_dest(t):
-        u = et * 3 + t
-        return u // 16, (u % 16) * 4 + kq
-
-    my_w, my_kq = et // 4, et % 4
-    src_et = (z * 16 + my_w) // 3
+        i, w = unit(t)
+        return i, place(i, w, groups_of(z, i)[0])
+
+    def unit_slot(t):
+        i, w = unit(t)
+        q, s = groups_of(z, i)
+        return gath.at[q, s, w // 8, w // 4 % 2, w // 2 % 2, w % 2], s
+
+    my_q, my_b = row_of(z, y)
+    my_xo = col_of(z, x)
+    my_w = my_xo // 2 * 8 + my_b * 4 + my_xo % 2 * 2 + c
 
     def unit_source(s):
-        return my_kq * 3 + s, src_et
+        return group(z, my_q, s), (z * 16 + my_w) // 3
 
     def far(n):
         return rem(y + 4 + (1 - 2 * (n % 2)) * ((n + 1) // 2), NY)
@@ -100,7 +136,7 @@
             [
                 (order_hbm, order_v),
                 (counts_hbm, counts_v),
-                (h_hbm, hbuf.at[z]),
+                (h_hbm, h_v),
                 (g_hbm, full.at[y, x, c]),
             ]
         )
@@ -123,23 +159,21 @@
     pos = lax.broadcasted_iota(jnp.int32, (128, 128), 0)
     expert = (pos >= counts_v[0:1, 0:1]).astype(F32)
     routed = jnp.sum(jnp.where(order == lane, expert, 0.0), axis=0, keepdims=True)
-    mbuf[z] = jnp.broadcast_to(routed, (16, 128)).astype(BF16)
-    h = hbuf[z].astype(F32)
+    h = h_v[...].astype(F32)
+    hbuf[z] = jnp.concatenate(
+        [h, jnp.zeros((8, 128), F32), jnp.broadcast_to(routed, (16, 128))], axis=0
+    ).astype(BF16)
     for k in range(2):
         hm[k] = jnp.where(routed == float(k), h, 0.0).astype(BF16)
         back[k] = jnp.zeros((168, 128), F32)
+        gwt[k] = jnp.zeros((2, 168, 256), F32)
 
     pl.semaphore_wait(bar, greeted)
 
-    g_own = full.at[y, x, c]
-
     def p_copy(t):
-        w = (et * 3 + t) % 16
-        return remote(
-            full.at[y, x, c, pl.ds(32 * t, 32)],
-            gath.at[kq // 2, kq % 2, ks, w // 2, w % 2],
-            p_s.at[t], p_r.at[ks], unit_dest(t),
-        )
+        dst, s = unit_slot(t)
+        src = full.at[y, x, c, pl.ds(32 * t, 32)]
+        return remote(src, dst, p_s.at[t], p_r.at[s], unit_dest(t))
 
     for t in range(3):
         own = is_self(unit_dest(t))
@@ -150,12 +184,11 @@
 
         @pl.when(own)
         def _():
-            w = (et * 3 + t) % 16
-            gath[kq // 2, kq % 2, ks, w // 2, w % 2] = full[y, x, c, pl.ds(32 * t, 32), :]
+            unit_slot(t)[0][...] = full[y, x, c, pl.ds(32 * t, 32), :]
 
     class Gather:
-        def __init__(self, block, pair, sems):
-            self.block, self.pair = block, pair
+        def __init__(self, block, pair, relayed, sems):
+            self.block, self.pair, self.relayed = block, pair, relayed
             self.ys, self.yr, self.xs, self.xr, self.cs, self.cr = sems
 
         def at(self, m, e):
@@ -181,6 +214,8 @@
 
             self.x_copy(m, 0, 0, 1).start()
             self.x_copy(m, 0, 1, -1).start()
+            if not self.relayed:
+                self.x_copy(m, 0, 2, 2).start()
 
         def relay(self, m):
             s = side(m)
@@ -189,7 +224,11 @@
 
         def finish(self, m):
             s = side(m)
-            self.x_copy(m, s, 1 - m % 2, s).wait_recv()
+            if self.relayed:
+                self.x_copy(m, s, 1 - m % 2, s).wait_recv()
+            else:
+                self.x_copy(m, -1, 0, 1).wait_recv()
+                self.x_copy(m, 1, 1, -1).wait_recv()
             self.x_copy(m, 2, 2, s).wait_recv()
             self.c_copy(m, c).start()
 
@@ -201,42 +240,50 @@
             s = side(m)
             self.x_copy(m, 0, 0, 1).wait_send()
             self.x_copy(m, 0, 1, -1).wait_send()
-            self.x_copy(m, -s, 2, s).wait_send()
+            if self.relayed:
+                self.x_copy(m, -s, 2, s).wait_send()
+            else:
+                self.x_copy(m, 0, 2, 2).wait_send()
             self.c_copy(m, c).wait_send()
 
     rows = Gather(
         lambda yy, xx: full.at[yy, xx, c],
         lambda yy, cc: full.at[yy, :, cc],
+        True,
         (a1y_s, a1y_r, a1x_s, a1x_r, a1c_s, a1c_r),
     )
+    def plane_block(yy, xx):
+        q, b = row_of(z, yy)
+        xo = col_of(z, xx)
+        return gath.at[q, :, xo // 2, b, xo % 2, c]
+
+    def plane_pair(yy, cc):
+        q, b = row_of(z, yy)
+        return gath.at[q, :, :, b, :, cc]
+
     plane = Gather(
-        lambda yy, xx: gath.at[xx % 2, c, :, yy, xx // 2],
-        lambda yy, cc: gath.at[:, cc, :, yy],
+        plane_block,
+        plane_pair,
+        False,
         (a2y_s, a2y_r, a2x_s, a2x_r, a2c_s, a2c_r),
     )
 
-    for d in (4, 3, 5, 2, 6, 1, 7):
+    for d in (1, 7, 2, 6, 3, 5, 4):
         rows.y_send(d).start()
 
     def hz(d, to, i):
         k = rem(z + d, NZ)
         return remote(hbuf.at[k], hbuf.at[k], hz_s.at[i], hz_r.at[i], zpeer(to))
 
-    def mz(d, to, i):
-        k = rem(z + d, NZ)
-        return remote(mbuf.at[k], mbuf.at[k], mz_s.at[i], mz_r.at[i], zpeer(to))
-
     direct = [(0, d, d % 12) for d in (3, -3, 2, -2, 1, -1)]
     relays = [(-3, d, d + 3) for d in (1, 2, 3)] + [(3, -d, 9 - d) for d in (1, 2)]
 
     def z_start(hops):
         for d, to, i in hops:
             hz(d, to, i).start()
-            mz(d, to, i).start()
 
     def z_recv(i):
         hz(-i, 1, i).wait_recv()
-        mz(-i, 1, i).wait_recv()
 
     z_start(direct)
 
@@ -309,16 +356,36 @@
 
             @pl.when(jnp.logical_not(is_self(unit_source(s))))
             def _():
-                blk = gath.at[my_kq // 2, my_kq % 2, s, my_w // 2, my_w % 2]
+                blk = gath.at[my_q, s, my_xo // 2, my_b, my_xo % 2, c]
                 remote(blk, blk, p_s.at[0], p_r.at[s], sibling).wait_recv()
 
-        for d in (4, 3, 5, 2, 6, 1, 7):
+        for d in (1, 7, 2, 6, 3, 5, 4):
             plane.y_send(d).start()
 
     def z_relay(m):
         z_recv(3)
         z_recv(9)
         z_start(relays)
+
+    def z_finish(m):
+        for i in (1, 2, 10, 11, 4, 5, 6, 7, 8):
+            z_recv(i)
+        for q in range(4):
+            for s in range(3):
+                block = hbuf[group(z, q, s)].astype(F32)
+                mask = block[176:177]
+                for k in range(2):
+                    hcat[q, k, :, 128 * s : 128 * s + 128] = jnp.where(
+                        mask == float(k), block[:168], 0.0
+                    ).astype(BF16)
+
+    def grad_weights(m):
+        plane.c_copy(m, 1 - c).wait_recv()
+        q, b = row_of(z, rem(y - near(m), NY))
+        g = [gath[q, s, :, b].reshape(256, 128) for s in range(3)]
+        g = jnp.concatenate(g, axis=1)
+        for k in range(2):
+            gwt[k, b] += dot(hcat[q, k], g, 1, 1)
 
     stages = [
         (0, 8, project),
@@ -327,13 +394,14 @@
         (3, 8, x_relay),
         (4, 8, rows.relay),
         (5, 8, x_sum),
+        (4, 1, z_relay),
+        (6, 1, plane_start),
         (6, 8, rows.finish),
-        (6, 1, plane_start),
-        (7, 1, z_relay),
         (8, 8, plane.forward),
-        (10, 8, plane.relay),
-        (12, 8, plane.finish),
-        (10, 8, grad_hidden),
+        (8, 8, grad_hidden),
+        (11, 1, z_finish),
+        (11, 8, plane.finish),
+        (12, 8, grad_weights),
     ]
 
     def step(n, carry):
@@ -355,19 +423,11 @@
         total = total + yr[d].astype(F32)
     out_ref[...] = total.astype(BF16)
 
-    for i in (1, 2, 10, 11, 4, 5, 6, 7, 8):
-        z_recv(i)
-    for i in range(12):
-        mask = mbuf[i].astype(F32)[0:1]
-        hi = hbuf[i].astype(F32)
-        for k in range(2):
-            hcat[k, :, 128 * i : 128 * i + 128] = jnp.where(mask == float(k), hi, 0.0).astype(BF16)
-    for m in range(8):
-        plane.c_copy(m, 1 - c).wait_recv()
-    gs = [gath[i // 6, (i // 3) % 2, i % 3].reshape(512, 128) for i in range(12)]
-    gs = jnp.concatenate(gs, axis=1)
     for k in range(2):
-        gw_ref[k] = dot(hcat[k], gs, 1, 1).astype(BF16)
+        for b in range(2):
+            for i in range(2):
+                cols = slice(256 * i + 128 * b, 256 * i + 128 * b + 128)
+                gw_ref[k, :, cols] = gwt[k, b, :, 128 * i : 128 * i + 128].astype(BF16)
 
     for t in range(3):
 
@@ -381,7 +441,6 @@
         ryf(d).wait_send()
     for d, to, i in direct + relays:
         hz(d, to, i).wait_send()
-        mz(d, to, i).wait_send()
 
     def drain(m, carry):
         rc(m).wait_send()
@@ -405,14 +464,14 @@
             jax.ShapeDtypeStruct((168, 128), BF16),
             jax.ShapeDtypeStruct((2, 168, 512), BF16),
         ),
-        in_specs=[pl.BlockSpec(memory_space=pl.ANY)] * 5,
+        in_specs=[pl.BlockSpec(memory_space=pltpu.HBM)] * 5,
         out_specs=(vmem, vmem, vmem),
         scratch_shapes=[
             pltpu.VMEM((8, 2, 168, 768), BF16),
             pltpu.VMEM((8, 4, 2, 96, 128), BF16),
-            pltpu.VMEM((2, 2, 3, 8, 2, 32, 128), BF16),
-            pltpu.VMEM((12, 168, 128), BF16),
-            pltpu.VMEM((12, 16, 128), BF16),
+            pltpu.VMEM((4, 3, 2, 2, 2, 2, 32, 128), BF16),
+            pltpu.VMEM((12, 192, 128), BF16),
+            pltpu.VMEM((168, 128), BF16),
             pltpu.VMEM((2, 168, 128), BF16),
             pltpu.VMEM((8, 4, 2, 96, 128), F32),
             pltpu.VMEM(blocks, BF16),
@@ -422,16 +481,17 @@
             pltpu.VMEM((8, 96, 128), BF16),
             pltpu.VMEM((8, 96, 128), BF16),
             pltpu.VMEM((2, 168, 128), F32),
-            pltpu.VMEM((2, 168, 1536), BF16),
+            pltpu.VMEM((4, 2, 168, 384), BF16),
+            pltpu.VMEM((2, 2, 168, 256), F32),
             pltpu.VMEM((1, 2), jnp.int32),
             pltpu.VMEM((1, 128), jnp.int32),
-            dma((8,)), dma((4,)), dma((3,)), dma((3,)), dma((12,)), dma((12,)), dma((12,)), dma((12,)),
+            dma((8,)), dma((4,)), dma((3,)), dma((3,)), dma((12,)), dma((12,)),
             dma((8,)), dma((8,)), dma((32,)), dma((32,)), dma((8,)), dma((8,)),
             dma((8,)), dma((8,)), dma((32,)), dma((32,)), dma((8,)), dma((8,)),
             dma((8,)), dma((8,)), dma((32,)), dma((32,)), dma((8,)), dma((8,)),
         ],
         compiler_params=pltpu.CompilerParams(
-            collective_id=0, has_side_effects=True, vmem_limit_bytes=48 << 20
+            collective_id=0, has_side_effects=True, vmem_limit_bytes=60 << 20
         ),
         name="moe_down",
     )(hidden_t, weights, grad_out_t, counts, row_order)

time: 66.1 us -> 59.9 us (0.906)
  Pallas kernels: 58.2 us -> 54.5 us
  local copies, waits for them, and re-layouts: 6.95 us -> 4.48 us
    pallas_call x1, Pallas kernels: 58.2 us -> 54.5 us  [shards(): pl.pallas_call(kernel, out_shape=(jax.ShapeDtypeStruct((96, 128), BF16),...]
    unnamed x13 -> x3, local copies, waits for them, and re-layouts: 6.95 us -> 4.48 us
where the time goes in v3:
time: 59.9 us; the launch traced here: 59.6 us
  Pallas kernels  54.5 us (91%)
  local copies, waits for them, and re-layouts  4.48 us (7%)
  between operations  0.64 us (1%)
    pallas_call x1, Pallas kernels, shards(): pl.pallas_call(kernel, out_shape=(jax.ShapeDtypeStruct((96, 128), BF16),...  54.5 us
    unnamed x3, local copies, waits for them, and re-layouts  4.48 us

profile of v3, /device:TPU:1, one launch (start us, length us, event | category | flops | bytes accessed | tf_op | source)
XLA Modules:
  0.0 59.6 jit_solution(11415983227145396881)
XLA Ops:
  0.6 54.5 %moe_down.1 = (bf16[96,128]{1,0:T(8,128)(2,1)}, bf16[168,128]{1,0:T(8,128)(2,1)}, bf16[2,168,512]{2,1,0:T(8,128)(2,1)}) custom-call(bf16[168,128]{1,0:T(8,128)(2,1)} %h_hbm.1, bf16[2,168,6144]{2,1,0:T(8,128)(2,1)} %w_hbm.1, bf16[96,128]{1,0:T(8,128)(2,1)} %g_hbm.1, s32[1,2]{1,0:T(1,128)} %counts_hbm.1, s32[1,128]{1,0:T(1,128)} %order_hbm.1), custom_call_target="tpu_custom_call" | custom-call | tf_op jit(solution)/shard_map/moe_down/pallas_call | solution.py:460
  55.1 1.3 %copy.11 = bf16[96,128]{1,0:T(8,128)(2,1)} copy(bf16[96,128]{1,0:T(8,128)(2,1)} %get-tuple-element.6) | data formatting | bytes 49152
  56.5 1.4 %copy.12 = bf16[168,128]{1,0:T(8,128)(2,1)} copy(bf16[168,128]{1,0:T(8,128)(2,1)} %get-tuple-element.7) | data formatting | bytes 86016
  57.9 1.7 %copy.13 = bf16[2,168,512]{2,1,0:T(8,128)(2,1)} copy(bf16[2,168,512]{2,1,0:T(8,128)(2,1)} %get-tuple-element.8) | data formatting | bytes 688128

commit v4 on v3

v4 whole, which is shorter than its diff:
```python
import jax
import jax.numpy as jnp
from jax import lax
from jax.experimental import pallas as pl
from jax.experimental.pallas import tpu as pltpu
from jax.sharding import PartitionSpec as P

MESH = pl.DeviceIdType.MESH
NY, NX, NZ = 8, 4, 12
BF16, F32 = jnp.bfloat16, jnp.float32


def dot(a, b, ca, cb):
    return lax.dot_general(a, b, (((ca,), (cb,)), ((), ())), preferred_element_type=F32)


def kernel(
    h_hbm, w_hbm, g_hbm, counts_hbm, order_hbm, out_ref, gh_ref, gw_ref,
    w_v, full, gath, hbuf, h_v, hm, part, sibs, sibr, xs, xr, ys, yr, back, hcat, gwt, counts_v, order_v,
    wsem, in_sem, p_s, p_r, hz_s, hz_r,
    a1y_s, a1y_r, a1x_s, a1x_r, a1c_s, a1c_r,
    a2y_s, a2y_r, a2x_s, a2x_r, a2c_s, a2c_r,
    rc_s, rc_r, rx_s, rx_r, ry_s, ry_r,
):
    z = lax.axis_index("dp")
    et = lax.axis_index("et")
    y, x, c = et // 8, (et // 2) % 4, et % 2

    def dev(yy, xx, cc):
        return (z, (yy * 4 + xx) * 2 + cc)

    def rem(a, n):
        return lax.rem(a + n, n)

    def ypeer(d):
        return dev(rem(y + d, NY), x, c)

    def xpeer(e):
        return dev(y, rem(x + e, NX), c)

    def zpeer(d):
        return (rem(z + d, NZ), et)

    sibling = dev(y, x, 1 - c)

    def remote(src, dst, ss, rs, peer):
        return pltpu.make_async_remote_copy(
            src_ref=src, dst_ref=dst, send_sem=ss, recv_sem=rs, device_id=peer, device_id_type=MESH
        )

    def corner(i):
        chip = i * 16 // 6
        return chip // 4, rem(chip % 4 - jnp.where(i % 3 == 0, 1, 0), NX)

    def groups_of(k, i):
        rel = rem(k - i, NZ) + 1
        return (rel // 3) % 4, rel % 3

    def group(i, q, s):
        return (i + 3 * q + s + 11) % NZ

    def place(i, w, q):
        yc, xc = corner(i)
        xo, b, cc = w // 8 * 2 + w // 2 % 2, w // 4 % 2, w % 2
        rank = jnp.where(q == 0, 3, jnp.where(q == 3, 2, 2 - q))
        yy = (yc + jnp.where(b == 1, 1 + rank, 8 - rank)) % NY
        return (yy * 4 + (xc + xo) % NX) * 2 + cc

    def row_of(i, yy):
        dy = rem(yy - corner(i)[0], NY)
        b = (dy + 3) % 8 // 4
        rank = jnp.where(b == 1, dy - 1, (8 - dy) % 8)
        return jnp.where(rank == 3, 0, jnp.where(rank == 2, 3, 2 - rank)), b

    def col_of(i, xx):
        return rem(xx - corner(i)[1], NX)

    def unit(t):
        u = et * 3 + t
        return u // 16, u % 16

    def unit_dest(t):
        i, w = unit(t)
        return i, place(i, w, groups_of(z, i)[0])

    def unit_slot(t):
        i, w = unit(t)
        q, s = groups_of(z, i)
        return gath.at[q, s, w // 8, w // 4 % 2, w // 2 % 2, w % 2], s

    my_q, my_b = row_of(z, y)
    my_xo = col_of(z, x)
    my_w = my_xo // 2 * 8 + my_b * 4 + my_xo % 2 * 2 + c

    def unit_source(s):
        return group(z, my_q, s), (z * 16 + my_w) // 3

    def far(n):
        return rem(y + 4 + (1 - 2 * (n % 2)) * ((n + 1) // 2), NY)

    def near(m):
        return ((m + 1) // 2) * (1 - 2 * ((m + 1) % 2))

    def side(m):
        return 1 - 2 * (m % 2)

    inputs = [
        pltpu.make_async_copy(src, dst, in_sem.at[i])
        for i, (src, dst) in enumerate(
            [
                (order_hbm, order_v),
                (counts_hbm, counts_v),
                (h_hbm, h_v),
                (g_hbm, full.at[y, x, c]),
            ]
        )
    ]
    for copy in inputs[::-1]:
        copy.start()

    def w_copy(n):
        yy = far(n)
        cols = pl.ds(pl.multiple_of(yy * 768, 768), 768)
        return pltpu.make_async_copy(w_hbm.at[:, :, cols], w_v.at[yy], wsem.at[n])

    for n in range(8):
        w_copy(n).start()

    bar = pltpu.get_barrier_semaphore()

    def greet(peer):
        pl.semaphore_signal(bar, inc=1, device_id=peer, device_id_type=MESH)

    def is_self(peer):
        return jnp.logical_and(peer[0] == z, peer[1] == et)

    greeted = 7 + 3 + 1 + 6
    for t in range(3):
        for peer in (unit_dest(t), unit_source(t)):
            own = is_self(peer)
            greeted = greeted + jnp.where(own, 0, 1)

            @pl.when(jnp.logical_not(own))
            def _():
                greet(peer)

    for d in (4, 3, 5, 2, 6, 1, 7):
        greet(ypeer(d))
    for d in (3, -3, 2, -2, 1, -1):
        greet(zpeer(d))
    for e in (1, 2, 3):
        greet(xpeer(e))
    greet(sibling)

    def p_copy(t):
        dst, s = unit_slot(t)
        src = full.at[y, x, c, pl.ds(32 * t, 32)]
        return remote(src, dst, p_s.at[t], p_r.at[s], unit_dest(t))

    class Gather:
        def __init__(self, block, pair, sems):
            self.block, self.pair = block, pair
            self.ys, self.yr, self.xs, self.xr, self.cs, self.cr = sems

        def at(self, m, e):
            return self.block(rem(y - near(m), NY), rem(x + e, NX))

        def y_send(self, d):
            blk = self.block(y, x)
            return remote(blk, blk, self.ys.at[d], self.yr.at[d], ypeer(d))

        def y_recv(self, m):
            d = rem(near(m), NY)
            blk = self.at(m, 0)
            remote(blk, blk, self.ys.at[d], self.yr.at[d], ypeer(d)).wait_recv()

        def x_copy(self, m, e, i, to):
            blk = self.at(m, e)
            return remote(blk, blk, self.xs.at[m * 4 + i], self.xr.at[m * 4 + i], xpeer(to))

        def forward(self, m):
            @pl.when(m > 0)
            def _():
                self.y_recv(m)

            self.x_copy(m, 0, 0, 1).start()
            self.x_copy(m, 0, 1, -1).start()
            self.x_copy(m, 0, 2, 2).start()

        def finish(self, m):
            self.x_copy(m, -1, 0, 1).wait_recv()
            self.x_copy(m, 1, 1, -1).wait_recv()
            self.x_copy(m, 2, 2, 2).wait_recv()
            self.c_copy(m, c).start()

        def c_copy(self, m, cc):
            blk = self.pair(rem(y - near(m), NY), cc)
            return remote(blk, blk, self.cs.at[m], self.cr.at[m], sibling)

        def drain(self, m):
            self.x_copy(m, 0, 0, 1).wait_send()
            self.x_copy(m, 0, 1, -1).wait_send()
            self.x_copy(m, 0, 2, 2).wait_send()
            self.c_copy(m, c).wait_send()

    class Ring:
        def x_copy(self, e, e_from):
            blk = full.at[y, rem(x - e_from, NX), c]
            return remote(blk, blk, a1x_s.at[e], a1x_r.at[e], xpeer(e))

        def y_copy(self, way, s, g, shift):
            yy = rem(y - way * (s + shift), NY)
            blk = full.at[yy, pl.ds(2 * g, 2), c]
            i = (4 if way < 0 else 0) + s
            return remote(blk, blk, a1y_s.at[i, g], a1y_r.at[i, g], ypeer(way))

        def c_copy(self, m, cc):
            blk = full.at[rem(y - near(m), NY), :, cc]
            return remote(blk, blk, a1c_s.at[m], a1c_r.at[m], sibling)

        def hops(self, s):
            return [(w, g) for g in range(2) for w in (1, -1) if s < 3 or (w > 0) == (g == 0)]

        def start(self):
            for e in (1, 3, 2):
                self.x_copy(e, 0).start()

        def level(self, s):
            if s == 0:
                for e in (1, 3, 2):
                    self.x_copy(e, e).wait_recv()
            if s < 4:
                for w, g in self.hops(s):
                    if s > 0:
                        self.y_copy(w, s - 1, g, 1).wait_recv()
                    self.y_copy(w, s, g, 0).start()
                if s == 3:
                    for w, g in self.hops(0):
                        if (w, g) not in self.hops(3):
                            self.y_copy(w, 2, g, 1).wait_recv()
            else:
                for w, g in self.hops(3):
                    self.y_copy(w, 3, g, 1).wait_recv()
            for m in {0: (0,), 4: (7,)}.get(s, (2 * s - 1, 2 * s)):
                self.c_copy(m, c).start()

        def drain(self):
            for e in (1, 3, 2):
                self.x_copy(e, 0).wait_send()
            for s in range(4):
                for w, g in self.hops(s):
                    self.y_copy(w, s, g, 0).wait_send()
            for m in range(8):
                self.c_copy(m, c).wait_send()

    rows = Ring()
    def plane_block(yy, xx):
        q, b = row_of(z, yy)
        xo = col_of(z, xx)
        return gath.at[q, :, xo // 2, b, xo % 2, c]

    def plane_pair(yy, cc):
        q, b = row_of(z, yy)
        return gath.at[q, :, :, b, :, cc]

    plane = Gather(
        plane_block,
        plane_pair,
        (a2y_s, a2y_r, a2x_s, a2x_r, a2c_s, a2c_r),
    )


    def hz(d, to, i):
        k = rem(z + d, NZ)
        return remote(hbuf.at[k], hbuf.at[k], hz_s.at[i], hz_r.at[i], zpeer(to))

    direct = [(0, d, d % 12) for d in (3, -3, 2, -2, 1, -1)]
    relays = [(-3, d, d + 3) for d in (1, 2, 3)] + [(3, -d, 9 - d) for d in (1, 2)]

    def z_start(hops):
        for d, to, i in hops:
            hz(d, to, i).start()

    def z_recv(i):
        hz(-i, 1, i).wait_recv()


    def rc(n):
        yy = far(n)
        return remote(sibs.at[yy], sibr.at[yy], rc_s.at[n], rc_r.at[n], sibling)

    def rx(n, i):
        yy, s = far(n), side(n)
        e, to = ((2, s), (-s, -s), (s, s))[i]
        j = n * 4 + i
        return remote(xs.at[yy, rem(x + e, NX)], xr.at[yy, i], rx_s.at[j], rx_r.at[j], xpeer(to))

    def ry(n):
        yy = far(n)
        d = rem(yy - y, NY)
        return remote(ys.at[yy], yr.at[d], ry_s.at[d], ry_r.at[d], dev(yy, x, c))

    def ryf(d):
        return remote(ys.at[y], yr.at[d], ry_s.at[d], ry_r.at[d], ypeer(d))

    def project(n):
        w_copy(n).wait()
        yy = far(n)
        p = dot(w_v[yy, 0], hm[0], 0, 0) + dot(w_v[yy, 1], hm[1], 0, 0)
        part[yy] = p.reshape(4, 2, 96, 128)
        sibs[yy] = part[yy, :, 1 - c].astype(BF16)

    def project_send(n):
        project(n)
        rc(n).start()

    def chip_sum(n):
        yy = far(n)
        rc(n).wait_recv()
        total = part[yy, :, c] + sibr[yy].astype(F32)
        part[yy, :, c] = total
        xs[yy] = total.astype(BF16)
        rx(n, 0).start()
        rx(n, 1).start()

    def x_relay(n):
        yy = far(n)
        e = rem(x + side(n), NX)
        rx(n, 0).wait_recv()
        xs[yy, e] = (part[yy, e, c] + xr[yy, 0].astype(F32)).astype(BF16)
        rx(n, 2).start()

    def x_sum(n):
        yy = far(n)
        rx(n, 1).wait_recv()
        rx(n, 2).wait_recv()
        total = part[yy, x, c] + xr[yy, 1].astype(F32) + xr[yy, 2].astype(F32)

        @pl.when(n < 7)
        def _():
            ys[yy] = total.astype(BF16)
            ry(n).start()

        @pl.when(n == 7)
        def _():
            part[yy, x, c] = total

    def grad_hidden(m):
        rows.c_copy(m, 1 - c).wait_recv()
        yy = rem(y - near(m), NY)
        g = full[yy].reshape(768, 128)
        for k in range(2):
            back[k] += dot(w_v[yy, k], g, 1, 0)

    def plane_start(m):
        for s in range(3):

            @pl.when(jnp.logical_not(is_self(unit_source(s))))
            def _():
                blk = gath.at[my_q, s, my_xo // 2, my_b, my_xo % 2, c]
                remote(blk, blk, p_s.at[0], p_r.at[s], sibling).wait_recv()

        for d in (1, 7, 2, 6, 3, 5, 4):
            plane.y_send(d).start()

    def z_relay(m):
        z_recv(3)
        z_recv(9)
        z_start(relays)

    def z_finish(q):
        for s in range(3):
            d = (3 * q + s + 11) % 12
            if d not in (0, 3, 9):
                z_recv(12 - d)
            block = hbuf[rem(z + d, NZ)].astype(F32)
            mask = block[176:177]
            for k in range(2):
                hcat[q, k, :, 128 * s : 128 * s + 128] = jnp.where(
                    mask == float(k), block[:168], 0.0
                ).astype(BF16)

    def grad_weights(m):
        plane.c_copy(m, 1 - c).wait_recv()
        q, b = row_of(z, rem(y - near(m), NY))
        g = [gath[q, s, :, b].reshape(256, 128) for s in range(3)]
        g = jnp.concatenate(g, axis=1)
        for k in range(2):
            gwt[k, b] += dot(hcat[q, k], g, 1, 1)

    inputs[3].wait()
    pl.semaphore_wait(bar, greeted)

    for t in range(3):
        own = is_self(unit_dest(t))

        @pl.when(jnp.logical_not(own))
        def _():
            p_copy(t).start()

        @pl.when(own)
        def _():
            unit_slot(t)[0][...] = full[y, x, c, pl.ds(32 * t, 32), :]

    rows.start()

    for copy in inputs[:3]:
        copy.wait()

    order = jnp.broadcast_to(order_v[...].astype(F32), (128, 128)).T
    lane = lax.broadcasted_iota(jnp.int32, (128, 128), 1).astype(F32)
    pos = lax.broadcasted_iota(jnp.int32, (128, 128), 0)
    expert = (pos >= counts_v[0:1, 0:1]).astype(F32)
    routed = jnp.sum(jnp.where(order == lane, expert, 0.0), axis=0, keepdims=True)
    h = h_v[...].astype(F32)
    hbuf[z] = jnp.concatenate(
        [h, jnp.zeros((8, 128), F32), jnp.broadcast_to(routed, (16, 128))], axis=0
    ).astype(BF16)
    for k in range(2):
        hm[k] = jnp.where(routed == float(k), h, 0.0).astype(BF16)
        back[k] = jnp.zeros((168, 128), F32)
        gwt[k] = jnp.zeros((2, 168, 256), F32)

    z_start(direct)

    order = [
        (project_send, 0), (project_send, 1), (project_send, 2), (chip_sum, 0), (project_send, 3),
        (chip_sum, 1), (chip_sum, 2), (rows.level, 0), (project_send, 4), (chip_sum, 3),
        (x_relay, 0), (project_send, 5), (x_relay, 1), (chip_sum, 4), (x_relay, 2),
        (project_send, 6), (plane_start, 0), (plane.forward, 0), (chip_sum, 5), (x_relay, 3),
        (x_sum, 0), (x_sum, 1), (rows.level, 1), (x_relay, 4), (project_send, 7), (chip_sum, 6),
        (plane.forward, 1), (plane.forward, 2), (x_sum, 2), (grad_hidden, 0), (x_relay, 5),
        (z_relay, 0), (chip_sum, 7), (plane.finish, 0), (x_sum, 3), (x_sum, 4),
        (plane.forward, 3), (plane.forward, 4), (z_finish, 0), (x_relay, 6), (grad_hidden, 1),
        (grad_hidden, 2), (plane.finish, 1), (plane.forward, 5), (plane.forward, 6),
        (z_finish, 1), (x_sum, 5), (plane.finish, 2), (x_relay, 7), (z_finish, 3),
        (plane.forward, 7), (plane.finish, 3), (x_sum, 6), (plane.finish, 4), (rows.level, 2),
        (plane.finish, 5), (x_sum, 7), (grad_hidden, 3), (plane.finish, 6), (grad_hidden, 4),
        (z_finish, 2), (plane.finish, 7), (grad_weights, 0), (rows.level, 3), (grad_weights, 1),
        (grad_weights, 2), (grad_weights, 3), (grad_weights, 4), (grad_weights, 5),
        (grad_weights, 6), (rows.level, 4), (grad_weights, 7), (grad_hidden, 5), (grad_hidden, 6),
        (grad_hidden, 7),
    ]
    for stage, index in order:
        stage(index)

    gh_ref[...] = jnp.where(routed == 0.0, back[0], back[1]).astype(BF16)

    total = part[y, x, c]
    for d in range(1, NY):
        ryf(d).wait_recv()
        total = total + yr[d].astype(F32)
    out_ref[...] = total.astype(BF16)

    for k in range(2):
        for b in range(2):
            for i in range(2):
                cols = slice(256 * i + 128 * b, 256 * i + 128 * b + 128)
                gw_ref[k, :, cols] = gwt[k, b, :, 128 * i : 128 * i + 128].astype(BF16)

    for t in range(3):

        @pl.when(jnp.logical_not(is_self(unit_dest(t))))
        def _():
            p_copy(t).wait_send()

    for d in range(1, NY):
        plane.y_send(d).wait_send()
        ryf(d).wait_send()
    for d, to, i in direct + relays:
        hz(d, to, i).wait_send()

    rows.drain()

    def drain(m, carry):
        rc(m).wait_send()
        plane.drain(m)
        for i in range(3):
            rx(m, i).wait_send()
        return carry

    lax.fori_loop(0, 8, drain, 0)


def write_out(*refs):
    for i in range(3):
        refs[3 + i][...] = refs[i][...]


def shards(hidden_t, weights, grad_out_t, counts, row_order):
    vmem = pl.BlockSpec(memory_space=pltpu.VMEM)
    dma = pltpu.SemaphoreType.DMA
    blocks = (8, 4, 96, 128)
    shapes = (
        jax.ShapeDtypeStruct((96, 128), BF16),
        jax.ShapeDtypeStruct((168, 128), BF16),
        jax.ShapeDtypeStruct((2, 168, 512), BF16),
    )
    results = pl.pallas_call(
        kernel,
        out_shape=shapes,
        in_specs=[pl.BlockSpec(memory_space=pltpu.HBM)] * 5,
        out_specs=(vmem, vmem, vmem),
        scratch_shapes=[
            pltpu.VMEM((8, 2, 168, 768), BF16),
            pltpu.VMEM((8, 4, 2, 96, 128), BF16),
            pltpu.VMEM((4, 3, 2, 2, 2, 2, 32, 128), BF16),
            pltpu.VMEM((12, 192, 128), BF16),
            pltpu.VMEM((168, 128), BF16),
            pltpu.VMEM((2, 168, 128), BF16),
            pltpu.VMEM((8, 4, 2, 96, 128), F32),
            pltpu.VMEM(blocks, BF16),
            pltpu.VMEM(blocks, BF16),
            pltpu.VMEM(blocks, BF16),
            pltpu.VMEM(blocks, BF16),
            pltpu.VMEM((8, 96, 128), BF16),
            pltpu.VMEM((8, 96, 128), BF16),
            pltpu.VMEM((2, 168, 128), F32),
            pltpu.VMEM((4, 2, 168, 384), BF16),
            pltpu.VMEM((2, 2, 168, 256), F32),
            pltpu.VMEM((1, 2), jnp.int32),
            pltpu.VMEM((1, 128), jnp.int32),
            dma((8,)), dma((4,)), dma((3,)), dma((3,)), dma((12,)), dma((12,)),
            dma((8, 2)), dma((8, 2)), dma((4,)), dma((4,)), dma((8,)), dma((8,)),
            dma((8,)), dma((8,)), dma((32,)), dma((32,)), dma((8,)), dma((8,)),
            dma((8,)), dma((8,)), dma((32,)), dma((32,)), dma((8,)), dma((8,)),
        ],
        compiler_params=pltpu.CompilerParams(
            collective_id=0, has_side_effects=True, vmem_limit_bytes=60 << 20
        ),
        name="moe_down",
    )(hidden_t, weights, grad_out_t, counts, row_order)
    return pl.pallas_call(
        write_out,
        out_shape=shapes,
        in_specs=[vmem] * 3,
        out_specs=(vmem,) * 3,
        name="write_out",
    )(*results)


def solution(mesh):
    in_specs = (P("et", "dp"), P(None, "et", None), P("et", "dp"), P("dp", None), P("dp", None))
    out_specs = (P("et", "dp"), P("et", "dp"), P(None, "et", "dp"))
    return jax.shard_map(shards, mesh=mesh, in_specs=in_specs, out_specs=out_specs, check_vma=False)
```

time: 59.9 us -> 54.6 us (0.912)
  local copies, waits for them, and re-layouts: 4.48 us -> 0 us
  Pallas kernels: 54.5 us -> 53.8 us
    unnamed x3 -> x0, local copies, waits for them, and re-layouts: 4.48 us -> none
    pallas_call x1 -> x2, Pallas kernels: 54.5 us -> 53.8 us  [the longest x1 52 us: shards(): pl.pallas_call(kernel, out_shape=shapes, in_specs=[pl.BlockSpec(memory_sp...]
where the time goes in v4:
time: 54.6 us; the launch traced here: 54.4 us
  Pallas kernels  53.8 us (99%)
  between operations  0.64 us (1%)
    pallas_call x1, Pallas kernels, shards(): pl.pallas_call(kernel, out_shape=shapes, in_specs=[pl.BlockSpec(memory_sp...  52 us
    pallas_call x1, Pallas kernels, shards(): pl.pallas_call(write_out, out_shape=shapes, in_specs=[vmem] * 3, out_spec...  1.78 us

profile of v4, /device:TPU:1, one launch (start us, length us, event | category | flops | bytes accessed | tf_op | source)
XLA Modules:
  0.0 54.4 jit_solution(13415657109393428679)
XLA Ops:
  0.6 52.0 %moe_down.1 = (bf16[96,128]{1,0:T(8,128)(2,1)}, bf16[168,128]{1,0:T(8,128)(2,1)}, bf16[2,168,512]{2,1,0:T(8,128)(2,1)}) custom-call(bf16[168,128]{1,0:T(8,128)(2,1)} %h_hbm.1, bf16[2,168,6144]{2,1,0:T(8,128)(2,1)} %w_hbm.1, bf16[96,128]{1,0:T(8,128)(2,1)} %g_hbm.1, s32[1,2]{1,0:T(1,128)} %counts_hbm.1, s32[1,128]{1,0:T(1,128)} %order_hbm.1), custom_call_target="tpu_custom_call" | custom-call | tf_op jit(solution)/shard_map/moe_down/pallas_call | solution.py:499
  52.6 1.8 %write_out.1 = (bf16[96,128]{1,0:T(8,128)(2,1)}, bf16[168,128]{1,0:T(8,128)(2,1)}, bf16[2,168,512]{2,1,0:T(8,128)(2,1)}) custom-call(bf16[96,128]{1,0:T(8,128)(2,1)} %get-tuple-element.6.refs_0_, bf16[168,128]{1,0:T(8,128)(2,1)} %get-tuple-element.7.refs_1_, bf16[2,168,512]{2,1,0:T(8,128)(2,1)} %get-tuple-element.8.refs_2_), custom_call_target="tpu_custom_call" | custom-call | tf_op jit(solution)/shard_map/write_out/pallas_call | solution.py:533

commit v5 on v4

--- a/solution.py
+++ b/solution.py
@@ -426,19 +426,19 @@
     order = [
         (project_send, 0), (project_send, 1), (project_send, 2), (chip_sum, 0), (project_send, 3),
         (chip_sum, 1), (chip_sum, 2), (rows.level, 0), (project_send, 4), (chip_sum, 3),
-        (x_relay, 0), (project_send, 5), (x_relay, 1), (chip_sum, 4), (x_relay, 2),
-        (project_send, 6), (plane_start, 0), (plane.forward, 0), (chip_sum, 5), (x_relay, 3),
-        (x_sum, 0), (x_sum, 1), (rows.level, 1), (x_relay, 4), (project_send, 7), (chip_sum, 6),
-        (plane.forward, 1), (plane.forward, 2), (x_sum, 2), (grad_hidden, 0), (x_relay, 5),
-        (z_relay, 0), (chip_sum, 7), (plane.finish, 0), (x_sum, 3), (x_sum, 4),
-        (plane.forward, 3), (plane.forward, 4), (z_finish, 0), (x_relay, 6), (grad_hidden, 1),
-        (grad_hidden, 2), (plane.finish, 1), (plane.forward, 5), (plane.forward, 6),
-        (z_finish, 1), (x_sum, 5), (plane.finish, 2), (x_relay, 7), (z_finish, 3),
-        (plane.forward, 7), (plane.finish, 3), (x_sum, 6), (plane.finish, 4), (rows.level, 2),
-        (plane.finish, 5), (x_sum, 7), (grad_hidden, 3), (plane.finish, 6), (grad_hidden, 4),
-        (z_finish, 2), (plane.finish, 7), (grad_weights, 0), (rows.level, 3), (grad_weights, 1),
-        (grad_weights, 2), (grad_weights, 3), (grad_weights, 4), (grad_weights, 5),
-        (grad_weights, 6), (rows.level, 4), (grad_weights, 7), (grad_hidden, 5), (grad_hidden, 6),
+        (x_relay, 0), (project_send, 5), (plane_start, 0), (plane.forward, 0), (chip_sum, 4),
+        (x_relay, 1), (x_relay, 2), (project_send, 6), (chip_sum, 5), (x_relay, 3), (x_sum, 0),
+        (plane.forward, 1), (plane.forward, 2), (rows.level, 1), (project_send, 7), (chip_sum, 6),
+        (plane.finish, 0), (x_relay, 4), (x_sum, 1), (x_sum, 2), (plane.forward, 3),
+        (plane.forward, 4), (z_relay, 0), (x_relay, 5), (z_finish, 0), (chip_sum, 7), (x_sum, 3),
+        (grad_hidden, 0), (grad_hidden, 1), (plane.forward, 5), (plane.forward, 6),
+        (plane.finish, 1), (x_relay, 6), (grad_hidden, 2), (x_sum, 4), (plane.finish, 2),
+        (z_finish, 1), (rows.level, 2), (plane.forward, 7), (plane.finish, 3), (z_finish, 3),
+        (x_sum, 5), (plane.finish, 4), (grad_hidden, 3), (x_relay, 7), (grad_hidden, 4),
+        (plane.finish, 5), (x_sum, 6), (plane.finish, 6), (rows.level, 3), (x_sum, 7),
+        (plane.finish, 7), (z_finish, 2), (grad_weights, 0), (grad_weights, 1), (grad_weights, 2),
+        (rows.level, 4), (grad_weights, 3), (grad_weights, 4), (grad_weights, 5),
+        (grad_weights, 6), (grad_weights, 7), (grad_hidden, 5), (grad_hidden, 6),
         (grad_hidden, 7),
     ]
     for stage, index in order:

time: 54.6 us -> 53.9 us (0.987)
  Pallas kernels: 53.8 us -> 53.1 us
    pallas_call x1, Pallas kernels: 52 us -> 51.3 us  [shards(): pl.pallas_call(kernel, out_shape=shapes, in_specs=[pl.BlockSpec(memory_sp...]
where the time goes in v5:
time: 53.9 us; the launch traced here: 53.7 us
  Pallas kernels  53.1 us (99%)
  between operations  0.64 us (1%)
    pallas_call x1, Pallas kernels, shards(): pl.pallas_call(kernel, out_shape=shapes, in_specs=[pl.BlockSpec(memory_sp...  51.3 us
    pallas_call x1, Pallas kernels, shards(): pl.pallas_call(write_out, out_shape=shapes, in_specs=[vmem] * 3, out_spec...  1.78 us

profile of v5, /device:TPU:1, one launch (start us, length us, event | category | flops | bytes accessed | tf_op | source)
XLA Modules:
  0.0 53.7 jit_solution(10200388778504821299)
XLA Ops:
  0.6 51.3 %moe_down.1 = (bf16[96,128]{1,0:T(8,128)(2,1)}, bf16[168,128]{1,0:T(8,128)(2,1)}, bf16[2,168,512]{2,1,0:T(8,128)(2,1)}) custom-call(bf16[168,128]{1,0:T(8,128)(2,1)} %h_hbm.1, bf16[2,168,6144]{2,1,0:T(8,128)(2,1)} %w_hbm.1, bf16[96,128]{1,0:T(8,128)(2,1)} %g_hbm.1, s32[1,2]{1,0:T(1,128)} %counts_hbm.1, s32[1,128]{1,0:T(1,128)} %order_hbm.1), custom_call_target="tpu_custom_call" | custom-call | tf_op jit(solution)/shard_map/moe_down/pallas_call | solution.py:499
  52.0 1.8 %write_out.1 = (bf16[96,128]{1,0:T(8,128)(2,1)}, bf16[168,128]{1,0:T(8,128)(2,1)}, bf16[2,168,512]{2,1,0:T(8,128)(2,1)}) custom-call(bf16[96,128]{1,0:T(8,128)(2,1)} %get-tuple-element.6.refs_0_, bf16[168,128]{1,0:T(8,128)(2,1)} %get-tuple-element.7.refs_1_, bf16[2,168,512]{2,1,0:T(8,128)(2,1)} %get-tuple-element.8.refs_2_), custom_call_target="tpu_custom_call" | custom-call | tf_op jit(solution)/shard_map/write_out/pallas_call | solution.py:533
